TPU v7x, 32 devices: a whole 2x2x4 slice. The times are simulated.
32 devices in a mesh: fiber: 8 (over z, y), group: 4 (over x, core).
Axes of the slice: x: 2, y: 2, z: 4, core: 2. Of those that a mesh axis runs over, the one named last changes fastest.
Arguments:
- tensor_slab: float32 [512, 32, 4096], P('fiber', None, 'group'), may hold values from -168 to 168
- start_matrix: float32 [512, 128], replicated, may hold values from -6 to 6
Outputs:
- triangle: float32 [512, 512], replicated
- subspace_basis: float32 [512, 128], replicated
- core_tensor: float32 [128, 32, 4096], P(None, 'fiber', 'group')
All inputs are finite; a program needn't handle non-finite values.
Results may differ from a plain program's by a relative error of at most 0.00016.
Values sent between devices are 32-bit elements; how exact they have to be, the bound alone decides.
A program may use at most 128 MiB of HBM per device.

v0:
```python
import jax
import jax.numpy as jnp
from jax import lax
from jax.sharding import PartitionSpec as P

ITERS = 2


HIGHEST = lax.Precision.HIGHEST


def product(left_side, right_side):
    return jnp.dot(left_side, right_side, precision=HIGHEST, preferred_element_type=jnp.float32)


def orthonormal(projected):
    small_gram = product(projected.T, projected)
    factor = jnp.linalg.cholesky(small_gram)
    return lax.linalg.triangular_solve(
        factor, projected, left_side=False, lower=True, transpose_a=True
    )


def shards(tensor_slab, start_matrix):
    unfolded = lax.all_to_all(tensor_slab, "fiber", split_axis=1, concat_axis=0, tiled=True)
    mode_rows = unfolded.shape[0]
    columns = unfolded.reshape(mode_rows, unfolded.shape[1] * unfolded.shape[2])
    column_scale = 1.0 / (tensor_slab.shape[1] * tensor_slab.shape[2] * lax.axis_size("group"))
    local_gram = (
        lax.dot_general(
            columns,
            columns,
            (((1,), (1,)), ((), ())),
            precision=HIGHEST,
            preferred_element_type=jnp.float32,
        )
        * column_scale
    )
    triangle = jnp.linalg.cholesky(lax.psum(local_gram, ("fiber", "group")))
    subspace_basis = start_matrix
    for iteration in range(ITERS):
        inner_part = product(triangle.T, subspace_basis)
        subspace_basis = orthonormal(product(triangle, inner_part))
    core_tensor = product(subspace_basis.T, columns)
    core_tensor = core_tensor.reshape(subspace_basis.shape[1], unfolded.shape[1], unfolded.shape[2])
    return (triangle, subspace_basis, core_tensor)


def solution(mesh):
    placed = (P("fiber", None, "group"), P())
    return jax.shard_map(
        shards,
        mesh=mesh,
        in_specs=placed,
        out_specs=(P(), P(), P(None, "fiber", "group")),
        check_vma=False,
    )
```

profile of v0, /device:TPU:1, one launch (start us, length us, event | category | flops | bytes accessed | tf_op | source)
XLA Modules:
  0.0 551.5 jit_solution(253346196833934887)
XLA Ops:
  7.2 8.3 %copy.20 = f32[64,32,1024]{2,0,1:T(8,128)S(1)} copy(f32[64,32,1024]{2,1,0:T(8,128)} %param.5) | data formatting | bytes 16777216 | tf_op args[0]
  15.5 188.5 %all_to_all.15 = f32[64,32,1024]{2,0,1:T(8,128)} all-to-all(f32[64,32,1024]{2,0,1:T(8,128)S(1)} %copy.20), channel_id=1, replica_groups=mesh['fiber'=8,'group'=4] {'fiber'}, dimensions={1} | all-to-all | bytes 16777216 | tf_op jit(solution)/shard_map/all_to_all | solution.py:25
  204.0 12.0 %copy.21 = f32[64,8,4,1024]{3,2,0,1:T(4,128)} copy(f32[64,8,4,1024]{3,0,2,1:T(8,128)} %bitcast.75) | data formatting | bytes 16777216 | tf_op jit(solution)/shard_map/all_to_all | solution.py:25
  216.0 24.5 %copy.30 = f32[64,8,4,1024]{3,1,2,0:T(8,128)S(1)} copy(f32[64,8,4,1024]{3,2,1,0:T(4,128)} %bitcast.76) | data formatting | bytes 16777216
  240.5 3.2 copy-done.1
  243.7 16.2 %convolution_multiply_fusion = f32[512,512]{0,1:T(8,128)} fusion(f32[512,4096]{1,0:T(8,128)S(1)} %bitcast.72), kind=kOutput, calls=%fused_computation | convolution fusion | flops 12885164032 | bytes 9437184 | tf_op jit(solution)/shard_map/dot_general | solution.py:30
  259.9 9.0 %copy.26 = f32[4096,512]{1,0:T(8,128)} copy(f32[4096,512]{0,1:T(8,128)} %bitcast.73) | data formatting | bytes 16777216 | tf_op jit(solution)/shard_map/dot_general | solution.py:13
  269.0 120.2 %all-reduce.3.cloned.1.call-done = f32[512,512]{0,1:T(8,128)} async-done(((f32[512,512]{0,1:T(8,128)}), f32[512,512]{0,1:T(8,128)}) %all-reduce.3.cloned.1.call-update) | async-done | bytes 1048592 | tf_op jit(solution)/shard_map/psum | solution.py:39
  389.1 1.6 copy.23
  392.2 11.7 %cholesky.120 = f32[128,128]{1,0:T(8,128)S(1)} custom-call(f32[128,128]{1,0:T(8,128)S(1)} %cholesky.330), custom_call_target="Cholesky" | custom-call | tf_op jit(solution)/shard_map/jit(cholesky)/cholesky | solution.py:39
  403.9 9.8 %custom-call.32 = f32[1,128,128]{1,2,0:T(8,128)S(1)} custom-call(f32[1,128,128]{2,1,0:T(8,128)S(1)} %get-tuple-element.23), custom_call_target="InvertDiagBlocksLowerTriangular" | custom-call | tf_op jit(solution)/shard_map/jit(cholesky)/cholesky | solution.py:39
  414.5 11.7 %cholesky.244 = f32[128,128]{1,0:T(8,128)S(1)} custom-call(f32[128,128]{1,0:T(8,128)S(1)} %cholesky.334), custom_call_target="Cholesky" | custom-call | tf_op jit(solution)/shard_map/jit(cholesky)/cholesky | solution.py:39
  426.3 10.2 %custom-call.33 = f32[1,128,128]{1,2,0:T(8,128)S(1)} custom-call(f32[1,128,128]{2,1,0:T(8,128)S(1)} %get-tuple-element.20), custom_call_target="InvertDiagBlocksLowerTriangular" | custom-call | tf_op jit(solution)/shard_map/jit(cholesky)/cholesky | solution.py:39
  437.1 11.7 %cholesky.265 = f32[128,128]{1,0:T(8,128)S(1)} custom-call(f32[128,128]{1,0:T(8,128)S(1)} %cholesky.339), custom_call_target="Cholesky" | custom-call | tf_op jit(solution)/shard_map/jit(cholesky)/cholesky | solution.py:39
  449.5 9.8 %custom-call.34 = f32[1,128,128]{1,2,0:T(8,128)S(1)} custom-call(f32[1,128,128]{2,1,0:T(8,128)S(1)} %get-tuple-element.17), custom_call_target="InvertDiagBlocksLowerTriangular" | custom-call | tf_op jit(solution)/shard_map/jit(cholesky)/cholesky | solution.py:39
  459.9 11.7 %cholesky.282 = f32[128,128]{1,0:T(8,128)S(1)} custom-call(f32[128,128]{1,0:T(8,128)S(1)} %convolution_subtract_fusion.2), custom_call_target="Cholesky" | custom-call | tf_op jit(solution)/shard_map/jit(cholesky)/cholesky | solution.py:39
  475.6 2.0 fusion.21
  479.3 11.7 %cholesky.310 = f32[128,128]{1,0:T(8,128)S(1)} custom-call(f32[128,128]{1,0:T(8,128)S(1)} %fusion.17), custom_call_target="Cholesky" | custom-call | tf_op jit(solution)/shard_map/jit(cholesky)/cholesky | solution.py:18
  492.4 9.8 %custom-call.36 = f32[1,128,128]{1,2,0:T(8,128)S(1)} custom-call(f32[1,128,128]{2,1,0:T(8,128)S(1)} %fusion.9), custom_call_target="InvertDiagBlocksLowerTriangular" | custom-call | tf_op jit(solution)/shard_map/triangular_solve/custom-call.8 | solution.py:19
  502.6 1.8 fusion.24
  506.3 11.7 %cholesky.321 = f32[128,128]{1,0:T(8,128)S(1)} custom-call(f32[128,128]{1,0:T(8,128)S(1)} %fusion.15), custom_call_target="Cholesky" | custom-call | tf_op jit(solution)/shard_map/jit(cholesky)/cholesky | solution.py:18
  519.4 9.8 %custom-call.37 = f32[1,128,128]{1,2,0:T(8,128)S(1)} custom-call(f32[1,128,128]{2,1,0:T(8,128)S(1)} %fusion.10), custom_call_target="InvertDiagBlocksLowerTriangular" | custom-call | tf_op jit(solution)/shard_map/triangular_solve/custom-call.8 | solution.py:19
  529.6 11.3 %fusion.2 = f32[128,4,1024]{2,0,1:T(8,128)S(1)} fusion(f32[4,1024,512]{2,1,0:T(8,128)} %bitcast.74, f32[128,512]{1,0:T(8,128)S(1)} %fusion.13), kind=kOutput, calls=%fused_computation.12 | convolution fusion | flops 3221225472 | bytes 10747904 | tf_op jit(solution)/shard_map/dot_general | solution.py:13
  540.9 2.7 copy.28
  (43 shorter events, 13.6 us)
Async XLA Ops:
  7.2 468.4 %copy-start = (f32[512,128]{1,0:T(8,128)S(1)}, f32[512,128]{1,0:T(8,128)}, u32[]{:S(2)}) copy-start(f32[512,128]{1,0:T(8,128)} %param.6) | copy-start | bytes 786436
  7.2 381.9 %all-reduce.3.cloned.1.call-start = ((), (), s32[]{:S(2)}) async-start(), calls=%async_computation.1 | async-start | bytes 2097152 | tf_op jit(solution)/shard_map/psum | solution.py:39
  240.5 3.2 copy-start.1
  475.6 65.3 %copy-start.2 = (f32[512,512]{1,0:T(8,128)}, f32[512,512]{1,0:T(8,128)S(1)}, u32[]{:S(2)}) copy-start(f32[512,512]{1,0:T(8,128)S(1)} %select_select_fusion) | copy-start | bytes 3145732
Sparse Core Ops, SparseCore 0:
  260.0 129.0 all-reduce.2
where the time goes:
time: 552 us; the launch traced here: 551 us
  blocking collectives  189 us (34%)
  other arithmetic  126 us (23%)
  waiting for transfers between devices  120 us (22%)
  local copies, waits for them, and re-layouts  62.4 us (11%)
  matrix products  37.3 us (7%)
  between operations  17.1 us (3%)
    all_to_all x1, blocking collectives, shards(): lax.all_to_all(tensor_slab, 'fiber', split_axis=1, concat_axis=0, tiled=T...  189 us
    psum x1, waiting for transfers between devices, shards(): triangle = jnp.linalg.cholesky(lax.psum(local_gram, ('fiber', 'group')))  120 us
    another operation x14, other arithmetic, shards(): triangle = jnp.linalg.cholesky(lax.psum(local_gram, ('fiber', 'group')))  78.7 us
    unnamed x10, local copies, waits for them, and re-layouts  39.4 us
    another operation x6, other arithmetic, orthonormal(): factor = jnp.linalg.cholesky(small_gram)  24.8 us
    another operation x4, other arithmetic, orthonormal(): lax.linalg.triangular_solve(factor, projected, left_side=False, lower=Tru...  20.9 us
    dot_general x7, matrix products, product(): jnp.dot(left_side, right_side, precision=HIGHEST, preferred_element_type=...  18.4 us
    dot_general x1, matrix products, shards(): lax.dot_general(columns, columns, (((1,), (1,)), ((), ())), precision=HIG...  16.2 us
  transfers between devices with their start and end apart: 1, of which 1 were waited for; matrix products, arithmetic and copies ran while one was open for 2% of the time, Pallas kernels for 0%

commit v1 on v0

v1 whole, which is shorter than its diff:
```python
import functools

import jax
import jax.numpy as jnp
from jax import lax
from jax.experimental import pallas as pl
from jax.experimental.pallas import tpu as pltpu
from jax.sharding import PartitionSpec as P

ITERS = 2
HIGHEST = lax.Precision.HIGHEST
BLOCK = 128
MESH = pl.DeviceIdType.MESH


def product(left_side, right_side):
    return jnp.dot(left_side, right_side, precision=HIGHEST, preferred_element_type=jnp.float32)


def dot_nt(a, b):
    return lax.dot_general(a, b, (((1,), (1,)), ((), ())), preferred_element_type=jnp.float32)


def split_two(value):
    high = value.astype(jnp.bfloat16)
    low = (value - high.astype(jnp.float32)).astype(jnp.bfloat16)
    return high, low


def exchange_kernel(
    nf, ng, chunks, per_slice, slices, width, rows, piece, scale,
    x_ref, high_ref, low_ref, gram_ref,
    xbuf, acc, packed, group_in, group_sum, fiber_in,
    own_sem, a_send, a_recv, g_send, g_recv, f_send, f_recv, fa_send, fa_recv, ga_send, ga_recv,
):
    mf = lax.axis_index("fiber")
    mg = lax.axis_index("group")
    barrier = pltpu.get_barrier_semaphore()
    for k in range(1, nf):
        pl.semaphore_signal(barrier, inc=1, device_id=(lax.rem(mf + k, nf), mg), device_id_type=MESH)
    for k in range(1, ng):
        pl.semaphore_signal(barrier, inc=1, device_id=(mf, lax.rem(mg + k, ng)), device_id_type=MESH)
    pl.semaphore_wait(barrier, nf + ng - 2)

    def slab_copy(c, k):
        peer = lax.rem(mf + k, nf)
        s, h = c // per_slice, c % per_slice
        return pltpu.make_async_remote_copy(
            src_ref=x_ref.at[peer * slices + s, :, pl.ds(pl.multiple_of(h * width, width), width)],
            dst_ref=xbuf.at[c, pl.ds(pl.multiple_of(mf * rows, rows), rows), :],
            send_sem=a_send.at[k - 1, c],
            recv_sem=a_recv.at[k - 1, c],
            device_id=(peer, mg),
            device_id_type=MESH,
        )

    def own_copy(c):
        s, h = c // per_slice, c % per_slice
        return pltpu.make_async_copy(
            x_ref.at[mf * slices + s, :, pl.ds(pl.multiple_of(h * width, width), width)],
            xbuf.at[c, pl.ds(pl.multiple_of(mf * rows, rows), rows), :],
            own_sem.at[c],
        )

    def start_chunk(c, _):
        for k in range(1, nf):
            slab_copy(c, k).start()
        own_copy(c).start()
        return 0

    lax.fori_loop(0, chunks, start_chunk, 0)
    acc[...] = jnp.zeros_like(acc)

    def use_chunk(c, _):
        own_copy(c).wait()
        for k in range(1, nf):
            slab_copy(c, k).wait_recv()
        high, low = split_two(xbuf[c])
        high_ref[c] = high
        low_ref[c] = low
        acc[...] += dot_nt(high, high) + (dot_nt(high, low) + dot_nt(low, high))
        return 0

    lax.fori_loop(0, chunks, use_chunk, 0)

    blocks = acc.shape[0] // BLOCK
    at = 0
    for i in range(blocks):
        for j in range(i + 1):
            packed[at * BLOCK:(at + 1) * BLOCK, :] = (
                acc[i * BLOCK:(i + 1) * BLOCK, j * BLOCK:(j + 1) * BLOCK] * scale
            )
            at += 1
    if at * BLOCK < packed.shape[0]:
        packed[at * BLOCK:, :] = jnp.zeros((packed.shape[0] - at * BLOCK, BLOCK), jnp.float32)

    big = piece * nf

    def group_copy(k):
        peer = lax.rem(mg + k, ng)
        return pltpu.make_async_remote_copy(
            src_ref=packed.at[pl.ds(pl.multiple_of(peer * big, 8), big), :],
            dst_ref=group_in.at[k - 1],
            send_sem=g_send.at[k - 1],
            recv_sem=g_recv.at[k - 1],
            device_id=(mf, peer),
            device_id_type=MESH,
        )

    for k in range(1, ng):
        group_copy(k).start()
    group_sum[...] = packed[pl.ds(pl.multiple_of(mg * big, 8), big), :]
    for k in range(1, ng):
        group_copy(k).wait_recv()
        group_sum[...] += group_in[k - 1]

    def fiber_copy(k):
        peer = lax.rem(mf + k, nf)
        return pltpu.make_async_remote_copy(
            src_ref=group_sum.at[pl.ds(pl.multiple_of(peer * piece, 8), piece), :],
            dst_ref=fiber_in.at[k - 1],
            send_sem=f_send.at[k - 1],
            recv_sem=f_recv.at[k - 1],
            device_id=(peer, mg),
            device_id_type=MESH,
        )

    for k in range(1, nf):
        fiber_copy(k).start()
    total = group_sum[pl.ds(pl.multiple_of(mf * piece, 8), piece), :]
    for k in range(1, nf):
        fiber_copy(k).wait_recv()
        total += fiber_in[k - 1]
    mine = pl.ds(pl.multiple_of(mg * big + mf * piece, 8), piece)
    gram_ref[mine, :] = total

    def fiber_gather(k):
        return pltpu.make_async_remote_copy(
            src_ref=gram_ref.at[mine, :],
            dst_ref=gram_ref.at[mine, :],
            send_sem=fa_send.at[k - 1],
            recv_sem=fa_recv.at[k - 1],
            device_id=(lax.rem(mf + k, nf), mg),
            device_id_type=MESH,
        )

    for k in range(1, nf):
        fiber_gather(k).start()
    for k in range(1, nf):
        fiber_gather(k).wait_recv()

    def group_gather(k):
        part = pl.ds(pl.multiple_of(mg * big, 8), big)
        return pltpu.make_async_remote_copy(
            src_ref=gram_ref.at[part, :],
            dst_ref=gram_ref.at[part, :],
            send_sem=ga_send.at[k - 1],
            recv_sem=ga_recv.at[k - 1],
            device_id=(mf, lax.rem(mg + k, ng)),
            device_id_type=MESH,
        )

    for k in range(1, ng):
        group_gather(k).start()
    for k in range(1, ng):
        group_gather(k).wait_recv()

    def end_chunk(c, _):
        for k in range(1, nf):
            slab_copy(c, k).wait_send()
        return 0

    lax.fori_loop(0, chunks, end_chunk, 0)
    for k in range(1, ng):
        group_copy(k).wait_send()
        group_gather(k).wait_send()
    for k in range(1, nf):
        fiber_copy(k).wait_send()
        fiber_gather(k).wait_send()


def exchange_and_gram(tensor_slab, nf, ng):
    rows, all_slices, cells = tensor_slab.shape
    slices = all_slices // nf
    modes = rows * nf
    width = 512 if cells % 512 == 0 else cells
    per_slice = cells // width
    chunks = slices * per_slice
    blocks = modes // BLOCK
    packed_rows = blocks * (blocks + 1) // 2 * BLOCK
    piece = -(-packed_rows // (nf * ng * 8)) * 8
    total_rows = piece * nf * ng
    scale = 1.0 / (all_slices * cells * ng)
    x = jnp.transpose(tensor_slab, (1, 0, 2))
    kernel = functools.partial(
        exchange_kernel, nf, ng, chunks, per_slice, slices, width, rows, piece, scale
    )
    dma = pltpu.SemaphoreType.DMA
    vmem = pl.BlockSpec(memory_space=pltpu.VMEM)
    high, low, gram = pl.pallas_call(
        kernel,
        out_shape=(
            jax.ShapeDtypeStruct((chunks, modes, width), jnp.bfloat16),
            jax.ShapeDtypeStruct((chunks, modes, width), jnp.bfloat16),
            jax.ShapeDtypeStruct((total_rows, BLOCK), jnp.float32),
        ),
        in_specs=[pl.BlockSpec(memory_space=pl.ANY)],
        out_specs=(vmem, vmem, vmem),
        scratch_shapes=[
            pltpu.VMEM((chunks, modes, width), jnp.float32),
            pltpu.VMEM((modes, modes), jnp.float32),
            pltpu.VMEM((total_rows, BLOCK), jnp.float32),
            pltpu.VMEM((ng - 1, piece * nf, BLOCK), jnp.float32),
            pltpu.VMEM((piece * nf, BLOCK), jnp.float32),
            pltpu.VMEM((nf - 1, piece, BLOCK), jnp.float32),
            dma((chunks,)),
            dma((nf - 1, chunks)),
            dma((nf - 1, chunks)),
            dma((ng - 1,)),
            dma((ng - 1,)),
            dma((nf - 1,)),
            dma((nf - 1,)),
            dma((nf - 1,)),
            dma((nf - 1,)),
            dma((ng - 1,)),
            dma((ng - 1,)),
        ],
        compiler_params=pltpu.CompilerParams(
            collective_id=0, has_side_effects=True, vmem_limit_bytes=56 * 1024 * 1024
        ),
    )(x)
    full = [[None] * blocks for _ in range(blocks)]
    at = 0
    for i in range(blocks):
        for j in range(i + 1):
            full[i][j] = gram[at * BLOCK:(at + 1) * BLOCK]
            if j < i:
                full[j][i] = full[i][j].T
            at += 1
    return high, low, jnp.block(full)


def project_kernel(per_slice, basis_ref, high_ref, low_ref, out_ref):
    b_high, b_low = split_two(basis_ref[...].T)
    width = high_ref.shape[2]

    def step(c, _):
        s, h = c // per_slice, c % per_slice
        high, low = high_ref[c], low_ref[c]
        value = jnp.dot(b_high, high, preferred_element_type=jnp.float32)
        value += jnp.dot(b_high, low, preferred_element_type=jnp.float32)
        value += jnp.dot(b_low, high, preferred_element_type=jnp.float32)
        out_ref[s, :, pl.ds(pl.multiple_of(h * width, width), width)] = value
        return 0

    lax.fori_loop(0, high_ref.shape[0], step, 0)


def project(basis, high, low, slices, cells):
    per_slice = cells // high.shape[2]
    vmem = pl.BlockSpec(memory_space=pltpu.VMEM)
    core = pl.pallas_call(
        functools.partial(project_kernel, per_slice),
        out_shape=jax.ShapeDtypeStruct((slices, basis.shape[1], cells), jnp.float32),
        in_specs=[vmem, vmem, vmem],
        out_specs=vmem,
        compiler_params=pltpu.CompilerParams(vmem_limit_bytes=56 * 1024 * 1024),
    )(basis, high, low)
    return jnp.transpose(core, (1, 0, 2))


def orthonormal(projected):
    small_gram = product(projected.T, projected)
    factor = jnp.linalg.cholesky(small_gram)
    return lax.linalg.triangular_solve(
        factor, projected, left_side=False, lower=True, transpose_a=True
    )


def shards(nf, ng, tensor_slab, start_matrix):
    high, low, gram = exchange_and_gram(tensor_slab, nf, ng)
    triangle = jnp.linalg.cholesky(gram)
    subspace_basis = start_matrix
    for iteration in range(ITERS):
        subspace_basis = orthonormal(product(gram, subspace_basis))
    core_tensor = project(
        subspace_basis, high, low, tensor_slab.shape[1] // nf, tensor_slab.shape[2]
    )
    return (triangle, subspace_basis, core_tensor)


def solution(mesh):
    placed = (P("fiber", None, "group"), P())
    return jax.shard_map(
        functools.partial(shards, mesh.shape["fiber"], mesh.shape["group"]),
        mesh=mesh,
        in_specs=placed,
        out_specs=(P(), P(), P(None, "fiber", "group")),
        check_vma=False,
    )
```

time: 552 us -> 394 us (0.71)
  Pallas kernels: 0 us -> 226 us
  blocking collectives: 189 us -> 0 us
  waiting for transfers between devices: 120 us -> 0 us
  local copies, waits for them, and re-layouts: 62.4 us -> 19.4 us
  matrix products: 37.3 us -> 11.9 us
  between operations: 17.1 us -> 3.99 us
    pallas_call x0 -> x2, Pallas kernels: none -> 226 us  [the longest x1 218 us: exchange_and_gram(): pl.pallas_call(kernel, out_shape=(jax.ShapeDtypeStruct((chunks, modes, wi...]
    all_to_all x1 -> x0, blocking collectives: 189 us -> none  [shards(): lax.all_to_all(tensor_slab, 'fiber', split_axis=1, concat_axis=0, tiled=T...]
    psum x1 -> x0, waiting for transfers between devices: 120 us -> none  [shards(): triangle = jnp.linalg.cholesky(lax.psum(local_gram, ('fiber', 'group')))]
    unnamed x10, local copies, waits for them, and re-layouts: 39.4 us -> 16 us
    dot_general x1 -> x0, matrix products: 16.2 us -> none  [shards(): lax.dot_general(columns, columns, (((1,), (1,)), ((), ())), precision=HIG...]
    dot_general x7 -> x4, matrix products: 18.4 us -> 4.96 us  [product(): jnp.dot(left_side, right_side, precision=HIGHEST, preferred_element_type=...]
    all_to_all x1 -> x0, local copies, waits for them, and re-layouts: 12 us -> none  [shards(): lax.all_to_all(tensor_slab, 'fiber', split_axis=1, concat_axis=0, tiled=T...]
    dot_general x3 -> x2, local copies, waits for them, and re-layouts: 9.22 us -> 0.18 us  [product(): jnp.dot(left_side, right_side, precision=HIGHEST, preferred_element_type=...]
  transfers between devices with their start and end apart: 1 -> 0, of which waited for: 1 -> 0; matrix products, arithmetic and copies ran while one was open for 2% -> 0% of each run, Pallas kernels for 0% -> 0%
where the time goes in v1:
time: 394 us; the launch traced here: 389 us
  Pallas kernels  226 us (57%)
  other arithmetic  127 us (32%)
  local copies, waits for them, and re-layouts  19.4 us (5%)
  matrix products  11.9 us (3%)
  between operations  3.99 us (1%)
    pallas_call x1, Pallas kernels, exchange_and_gram(): pl.pallas_call(kernel, out_shape=(jax.ShapeDtypeStruct((chunks, modes, wi...  218 us
    another operation x15, other arithmetic, shards(): triangle = jnp.linalg.cholesky(gram)  79.3 us
    another operation x6, other arithmetic, orthonormal(): factor = jnp.linalg.cholesky(small_gram)  24.8 us
    another operation x4, other arithmetic, orthonormal(): lax.linalg.triangular_solve(factor, projected, left_side=False, lower=Tru...  20.9 us
    unnamed x10, local copies, waits for them, and re-layouts  16 us
    pallas_call x1, Pallas kernels, project(): pl.pallas_call(functools.partial(project_kernel, per_slice), out_shape=ja...  8.27 us

profile of v1, /device:TPU:1, one launch (start us, length us, event | category | flops | bytes accessed | tf_op | source)
XLA Modules:
  0.0 389.0 jit_solution(5476800189378834960)
XLA Ops:
  0.6 11.5 %copy.23 = f32[64,32,1024]{2,0,1:T(8,128)} copy(f32[64,32,1024]{2,1,0:T(8,128)} %param.5) | data formatting | bytes 16777216 | tf_op args[0]
  12.1 218.1 %shard_map.49 = (bf16[8,512,512]{2,1,0:T(8,128)(2,1)}, bf16[8,512,512]{2,1,0:T(8,128)(2,1)}, f32[1280,128]{1,0:T(8,128)}) custom-call(f32[32,64,1024]{2,1,0:T(8,128)} %bitcast.70), custom_call_target="tpu_custom_call" | custom-call | tf_op jit(solution)/shard_map/pallas_call | solution.py:200
  231.3 1.3 copy.6
  233.5 1.8 fusion.19
  236.0 11.7 %cholesky.310 = f32[128,128]{1,0:T(8,128)S(1)} custom-call(f32[128,128]{1,0:T(8,128)S(1)} %fusion.14), custom_call_target="Cholesky" | custom-call | tf_op jit(solution)/shard_map/jit(cholesky)/cholesky | solution.py:274
  249.0 9.8 %custom-call.36 = f32[1,128,128]{1,2,0:T(8,128)S(1)} custom-call(f32[1,128,128]{2,1,0:T(8,128)S(1)} %fusion.7), custom_call_target="InvertDiagBlocksLowerTriangular" | custom-call | tf_op jit(solution)/shard_map/triangular_solve/custom-call.8 | solution.py:275
  259.3 1.8 fusion.21
  263.4 11.7 %cholesky.321 = f32[128,128]{1,0:T(8,128)S(1)} custom-call(f32[128,128]{1,0:T(8,128)S(1)} %fusion.12), custom_call_target="Cholesky" | custom-call | tf_op jit(solution)/shard_map/jit(cholesky)/cholesky | solution.py:274
  276.4 9.8 %custom-call.37 = f32[1,128,128]{1,2,0:T(8,128)S(1)} custom-call(f32[1,128,128]{2,1,0:T(8,128)S(1)} %fusion.8), custom_call_target="InvertDiagBlocksLowerTriangular" | custom-call | tf_op jit(solution)/shard_map/triangular_solve/custom-call.8 | solution.py:275
  286.2 1.1 convolution_bitcast_fusion.basis_ref
  287.3 8.3 %shard_map.50 = f32[4,128,1024]{2,1,0:T(8,128)} custom-call(f32[512,128]{1,0:T(8,128)} %convolution_bitcast_fusion.basis_ref, bf16[8,512,512]{2,1,0:T(8,128)(2,1)} %get-tuple-element.9.high_ref, bf16[8,512,512]{2,1,0:T(8,128)(2,1)} %get-tuple-element.10.low_ref), custom_call_target="tpu_custom_call" | custom-call | tf_op jit(solution)/shard_map/pallas_call | solution.py:262
  295.6 4.3 %copy.20 = f32[128,4,1024]{2,1,0:T(4,128)} copy(f32[128,4,1024]{2,0,1:T(8,128)} %bitcast.71) | data formatting | bytes 4194304
  299.8 11.7 %cholesky.120 = f32[128,128]{1,0:T(8,128)S(1)} custom-call(f32[128,128]{1,0:T(8,128)S(1)} %cholesky.330), custom_call_target="Cholesky" | custom-call | tf_op jit(solution)/shard_map/jit(cholesky)/cholesky | solution.py:282
  312.3 9.8 %custom-call.32 = f32[1,128,128]{1,2,0:T(8,128)S(1)} custom-call(f32[1,128,128]{2,1,0:T(8,128)S(1)} %get-tuple-element.39), custom_call_target="InvertDiagBlocksLowerTriangular" | custom-call | tf_op jit(solution)/shard_map/jit(cholesky)/cholesky | solution.py:282
  322.2 1.2 constant_dynamic-update-slice_fusion.2
  323.5 1.3 convolution_subtract_fusion
  324.8 11.7 %cholesky.244 = f32[128,128]{1,0:T(8,128)S(1)} custom-call(f32[128,128]{1,0:T(8,128)S(1)} %cholesky.334), custom_call_target="Cholesky" | custom-call | tf_op jit(solution)/shard_map/jit(cholesky)/cholesky | solution.py:282
  338.4 10.0 %custom-call.33 = f32[1,128,128]{1,2,0:T(8,128)S(1)} custom-call(f32[1,128,128]{2,1,0:T(8,128)S(1)} %get-tuple-element.36), custom_call_target="InvertDiagBlocksLowerTriangular" | custom-call | tf_op jit(solution)/shard_map/jit(cholesky)/cholesky | solution.py:282
  348.7 1.3 convolution_subtract_fusion.1
  350.0 11.7 %cholesky.265 = f32[128,128]{1,0:T(8,128)S(1)} custom-call(f32[128,128]{1,0:T(8,128)S(1)} %cholesky.339), custom_call_target="Cholesky" | custom-call | tf_op jit(solution)/shard_map/jit(cholesky)/cholesky | solution.py:282
  363.2 9.8 %custom-call.34 = f32[1,128,128]{1,2,0:T(8,128)S(1)} custom-call(f32[1,128,128]{2,1,0:T(8,128)S(1)} %get-tuple-element.33), custom_call_target="InvertDiagBlocksLowerTriangular" | custom-call | tf_op jit(solution)/shard_map/jit(cholesky)/cholesky | solution.py:282
  373.2 1.2 convolution_subtract_fusion.2
  374.4 11.7 %cholesky.282 = f32[128,128]{1,0:T(8,128)S(1)} custom-call(f32[128,128]{1,0:T(8,128)S(1)} %convolution_subtract_fusion.2), custom_call_target="Cholesky" | custom-call | tf_op jit(solution)/shard_map/jit(cholesky)/cholesky | solution.py:282
  387.5 1.1 select_select_fusion
  (45 shorter events, 11.3 us)
Async XLA Ops:
  0.6 232.8 %copy-start = (f32[512,128]{1,0:T(8,128)S(1)}, f32[512,128]{1,0:T(8,128)}, u32[]{:S(2)}) copy-start(f32[512,128]{1,0:T(8,128)} %param.6) | copy-start | bytes 786436
  232.6 0.6 copy-start.2
  232.8 0.6 copy-start.3
  262.5 37.4 %copy-start.1 = (f32[512,512]{1,0:T(8,128)}, f32[512,512]{1,0:T(8,128)S(1)}, u32[]{:S(2)}) copy-start(f32[512,512]{1,0:T(8,128)S(1)} %fusion) | copy-start | bytes 3145732

commit v2 on v1

--- a/solution.py
+++ b/solution.py
@@ -240,8 +240,92 @@
     return high, low, jnp.block(full)
 
 
-def project_kernel(per_slice, basis_ref, high_ref, low_ref, out_ref):
-    b_high, b_low = split_two(basis_ref[...].T)
+def dot_tn(a, b):
+    return lax.dot_general(
+        a, b, (((0,), (0,)), ((), ())), precision=HIGHEST, preferred_element_type=jnp.float32
+    )
+
+
+def product_nt(a, b):
+    return lax.dot_general(
+        a, b, (((1,), (1,)), ((), ())), precision=HIGHEST, preferred_element_type=jnp.float32
+    )
+
+
+def factor_many(matrices):
+    n = BLOCK
+    row = lax.broadcasted_iota(jnp.int32, (n, n), 0)
+    col = lax.broadcasted_iota(jnp.int32, (n, n), 1)
+    eye = jnp.where(row == col, 1.0, 0.0).astype(jnp.float32)
+    rest = [jnp.concatenate([m, eye], axis=1) for m in matrices]
+    done = [[] for _ in matrices]
+    for k in range(n // 8):
+        panels = [w[:8] for w in rest]
+        corners = [
+            [jnp.broadcast_to(p[:, 8 * k + t:8 * k + t + 1], (8, n)) for t in range(8)]
+            for p in panels
+        ]
+        rows = [[] for _ in matrices]
+        for t in range(8):
+            for q in range(len(matrices)):
+                pivot = corners[q][t][t:t + 1]
+                inverse = lax.rsqrt(pivot)
+                c = corners[q][t] * inverse
+                for v in range(t + 1, 8):
+                    corners[q][v] = corners[q][v] - c * c[v:v + 1]
+                wide = jnp.concatenate([inverse, inverse], axis=1)
+                r = panels[q][t:t + 1] * wide
+                rows[q].append(r)
+                panels[q] = panels[q] - jnp.concatenate([c, c], axis=1) * r
+        for q in range(len(matrices)):
+            panel = jnp.concatenate(rows[q], axis=0)
+            done[q].append(panel)
+            if 8 * (k + 1) < n:
+                update = dot_tn(panel[:, :n], panel)
+                rest[q] = rest[q][8:] - update[8 * (k + 1):]
+    result = []
+    for q in range(len(matrices)):
+        both = jnp.concatenate(done[q], axis=0)
+        lower = jnp.where(row >= col, both[:, :n].T, 0.0)
+        result.append((lower, both[:, n:]))
+    return result
+
+
+def factor_kernel(per_slice, start_ref, gram_ref, high_ref, low_ref, tri_ref, basis_ref, core_ref, work):
+    modes = gram_ref.shape[0]
+    blocks = modes // BLOCK
+    work[...] = gram_ref[...]
+    tri_ref[...] = jnp.zeros_like(tri_ref)
+    basis = start_ref[...].T
+
+    def projected_gram(basis):
+        projected = product(basis, gram_ref[...])
+        return projected, product_nt(projected, projected)
+
+    projected, small = projected_gram(basis)
+    for i in range(max(blocks, ITERS)):
+        matrices = []
+        if i < blocks:
+            lo = i * BLOCK
+            matrices.append(work[lo:lo + BLOCK, lo:lo + BLOCK])
+        if i < ITERS:
+            matrices.append(small)
+        factors = factor_many(matrices)
+        if i < ITERS:
+            basis = product(factors[-1][1], projected)
+            if i + 1 < ITERS:
+                projected, small = projected_gram(basis)
+            else:
+                basis_ref[...] = basis.T
+        if i < blocks:
+            lower, inverse = factors[0]
+            tri_ref[lo:lo + BLOCK, lo:lo + BLOCK] = lower
+            if i + 1 < blocks:
+                below = product_nt(work[lo + BLOCK:, lo:lo + BLOCK], inverse)
+                tri_ref[lo + BLOCK:, lo:lo + BLOCK] = below
+                work[lo + BLOCK:, lo + BLOCK:] = work[lo + BLOCK:, lo + BLOCK:] - product_nt(below, below)
+
+    b_high, b_low = split_two(basis)
     width = high_ref.shape[2]
 
     def step(c, _):
@@ -250,43 +334,30 @@
         value = jnp.dot(b_high, high, preferred_element_type=jnp.float32)
         value += jnp.dot(b_high, low, preferred_element_type=jnp.float32)
         value += jnp.dot(b_low, high, preferred_element_type=jnp.float32)
-        out_ref[s, :, pl.ds(pl.multiple_of(h * width, width), width)] = value
+        core_ref[s, :, pl.ds(pl.multiple_of(h * width, width), width)] = value
         return 0
 
     lax.fori_loop(0, high_ref.shape[0], step, 0)
-
-
-def project(basis, high, low, slices, cells):
-    per_slice = cells // high.shape[2]
-    vmem = pl.BlockSpec(memory_space=pltpu.VMEM)
-    core = pl.pallas_call(
-        functools.partial(project_kernel, per_slice),
-        out_shape=jax.ShapeDtypeStruct((slices, basis.shape[1], cells), jnp.float32),
-        in_specs=[vmem, vmem, vmem],
-        out_specs=vmem,
-        compiler_params=pltpu.CompilerParams(vmem_limit_bytes=56 * 1024 * 1024),
-    )(basis, high, low)
-    return jnp.transpose(core, (1, 0, 2))
-
-
-def orthonormal(projected):
-    small_gram = product(projected.T, projected)
-    factor = jnp.linalg.cholesky(small_gram)
-    return lax.linalg.triangular_solve(
-        factor, projected, left_side=False, lower=True, transpose_a=True
-    )
 
 
 def shards(nf, ng, tensor_slab, start_matrix):
     high, low, gram = exchange_and_gram(tensor_slab, nf, ng)
-    triangle = jnp.linalg.cholesky(gram)
-    subspace_basis = start_matrix
-    for iteration in range(ITERS):
-        subspace_basis = orthonormal(product(gram, subspace_basis))
-    core_tensor = project(
-        subspace_basis, high, low, tensor_slab.shape[1] // nf, tensor_slab.shape[2]
-    )
-    return (triangle, subspace_basis, core_tensor)
+    slices, cells = tensor_slab.shape[1] // nf, tensor_slab.shape[2]
+    modes, rank = start_matrix.shape
+    vmem = pl.BlockSpec(memory_space=pltpu.VMEM)
+    triangle, basis, core = pl.pallas_call(
+        functools.partial(factor_kernel, cells // high.shape[2]),
+        out_shape=(
+            jax.ShapeDtypeStruct((modes, modes), jnp.float32),
+            jax.ShapeDtypeStruct((modes, rank), jnp.float32),
+            jax.ShapeDtypeStruct((slices, rank, cells), jnp.float32),
+        ),
+        in_specs=[vmem] * 4,
+        out_specs=(vmem, vmem, vmem),
+        scratch_shapes=[pltpu.VMEM((modes, modes), jnp.float32)],
+        compiler_params=pltpu.CompilerParams(vmem_limit_bytes=56 * 1024 * 1024),
+    )(start_matrix, gram, high, low)
+    return (triangle, basis, jnp.transpose(core, (1, 0, 2)))
 
 
 def solution(mesh):

time: 394 us -> 285 us (0.72); the launches traced: 389 us -> 285 us
  other arithmetic: 127 us -> 1.1 us
  Pallas kernels: 226 us -> 264 us
  matrix products: 11.9 us -> 0 us
    another operation x25 -> x0, other arithmetic: 125 us -> none  [the longest x15 79.3 us: shards(): triangle = jnp.linalg.cholesky(gram)]
    pallas_call x1, Pallas kernels: 8.27 us -> 46.5 us  [shards(): pl.pallas_call(functools.partial(factor_kernel, cells // high.shape[2]),...]
    another operation x8 -> x0, matrix products: 6.95 us -> none  [the longest x6 5.46 us: shards(): triangle = jnp.linalg.cholesky(gram)]
    dot_general x4 -> x0, matrix products: 4.96 us -> none  [product(): jnp.dot(left_side, right_side, precision=HIGHEST, preferred_element_type=...]
    unnamed x10 -> x2, local copies, waits for them, and re-layouts: 16 us -> 15.7 us
where the time goes in v2:
time: 285 us
  Pallas kernels  264 us (93%)
  local copies, waits for them, and re-layouts  18.5 us (6%)
    pallas_call x1, Pallas kernels, exchange_and_gram(): pl.pallas_call(kernel, out_shape=(jax.ShapeDtypeStruct((chunks, modes, wi...  218 us
    pallas_call x1, Pallas kernels, shards(): pl.pallas_call(functools.partial(factor_kernel, cells // high.shape[2]),...  46.5 us
    unnamed x2, local copies, waits for them, and re-layouts  15.7 us

profile of v2, /device:TPU:1, one launch (start us, length us, event | category | flops | bytes accessed | tf_op | source)
XLA Modules:
  0.0 284.6 jit_solution(579285426742129630)
XLA Ops:
  0.6 11.5 %copy.16 = f32[64,32,1024]{2,0,1:T(8,128)} copy(f32[64,32,1024]{2,1,0:T(8,128)} %param.2) | data formatting | bytes 16777216 | tf_op args[0]
  12.1 217.8 %shard_map.49 = (bf16[8,512,512]{2,1,0:T(8,128)(2,1)}, bf16[8,512,512]{2,1,0:T(8,128)(2,1)}, f32[1280,128]{1,0:T(8,128)}) custom-call(f32[32,64,1024]{2,1,0:T(8,128)} %bitcast.16), custom_call_target="tpu_custom_call" | custom-call | tf_op jit(solution)/shard_map/pallas_call | solution.py:200
  229.9 1.3 copy.6
  231.3 1.1 slice_bitcast_fusion.5
  232.4 0.1 copy.10
  232.5 0.1 copy.12
  232.6 0.1 copy.11
  232.7 0.1 copy.13
  232.9 1.1 maximum_maximum_fusion.gram_ref
  233.9 46.5 %shard_map.50 = (f32[512,512]{1,0:T(8,128)}, f32[512,128]{1,0:T(8,128)}, f32[4,128,1024]{2,1,0:T(8,128)}) custom-call(f32[512,128]{1,0:T(8,128)} %start_ref.1, f32[512,512]{1,0:T(8,128)} %maximum_maximum_fusion.gram_ref, bf16[8,512,512]{2,1,0:T(8,128)(2,1)} %get-tuple-element.10.high_ref, bf16[8,512,512]{2,1,0:T(8,128)(2,1)} %get-tuple-element.11.low_ref), custom_call_target="tpu_custom_call" | custom-call | tf_op jit(solution)/shard_map/pallas_call | solution.py:348
  280.4 4.3 %copy.14 = f32[128,4,1024]{2,1,0:T(4,128)} copy(f32[128,4,1024]{2,0,1:T(8,128)} %bitcast.17) | data formatting | bytes 4194304
  (2 shorter events, 0.1 us)

commit v3 on v2

--- a/solution.py
+++ b/solution.py
@@ -46,7 +46,7 @@
         peer = lax.rem(mf + k, nf)
         s, h = c // per_slice, c % per_slice
         return pltpu.make_async_remote_copy(
-            src_ref=x_ref.at[peer * slices + s, :, pl.ds(pl.multiple_of(h * width, width), width)],
+            src_ref=x_ref.at[:, peer * slices + s, pl.ds(pl.multiple_of(h * width, width), width)],
             dst_ref=xbuf.at[c, pl.ds(pl.multiple_of(mf * rows, rows), rows), :],
             send_sem=a_send.at[k - 1, c],
             recv_sem=a_recv.at[k - 1, c],
@@ -57,7 +57,7 @@
     def own_copy(c):
         s, h = c // per_slice, c % per_slice
         return pltpu.make_async_copy(
-            x_ref.at[mf * slices + s, :, pl.ds(pl.multiple_of(h * width, width), width)],
+            x_ref.at[:, mf * slices + s, pl.ds(pl.multiple_of(h * width, width), width)],
             xbuf.at[c, pl.ds(pl.multiple_of(mf * rows, rows), rows), :],
             own_sem.at[c],
         )
@@ -191,7 +191,6 @@
     piece = -(-packed_rows // (nf * ng * 8)) * 8
     total_rows = piece * nf * ng
     scale = 1.0 / (all_slices * cells * ng)
-    x = jnp.transpose(tensor_slab, (1, 0, 2))
     kernel = functools.partial(
         exchange_kernel, nf, ng, chunks, per_slice, slices, width, rows, piece, scale
     )
@@ -228,16 +227,8 @@
         compiler_params=pltpu.CompilerParams(
             collective_id=0, has_side_effects=True, vmem_limit_bytes=56 * 1024 * 1024
         ),
-    )(x)
-    full = [[None] * blocks for _ in range(blocks)]
-    at = 0
-    for i in range(blocks):
-        for j in range(i + 1):
-            full[i][j] = gram[at * BLOCK:(at + 1) * BLOCK]
-            if j < i:
-                full[j][i] = full[i][j].T
-            at += 1
-    return high, low, jnp.block(full)
+    )(tensor_slab)
+    return high, low, gram
 
 
 def dot_tn(a, b):
@@ -291,15 +282,24 @@
     return result
 
 
-def factor_kernel(per_slice, start_ref, gram_ref, high_ref, low_ref, tri_ref, basis_ref, core_ref, work):
-    modes = gram_ref.shape[0]
+def factor_kernel(per_slice, start_ref, gram_ref, high_ref, low_ref, tri_ref, basis_ref, core_ref, full, work):
+    modes = full.shape[0]
     blocks = modes // BLOCK
-    work[...] = gram_ref[...]
+    at = 0
+    for i in range(blocks):
+        for j in range(i + 1):
+            block = gram_ref[at * BLOCK:(at + 1) * BLOCK, :]
+            across, down = pl.ds(i * BLOCK, BLOCK), pl.ds(j * BLOCK, BLOCK)
+            full[across, down] = block
+            work[across, down] = block
+            if j < i:
+                full[down, across] = block.T
+            at += 1
     tri_ref[...] = jnp.zeros_like(tri_ref)
     basis = start_ref[...].T
 
     def projected_gram(basis):
-        projected = product(basis, gram_ref[...])
+        projected = product(basis, full[...])
         return projected, product_nt(projected, projected)
 
     projected, small = projected_gram(basis)
@@ -328,16 +328,13 @@
     b_high, b_low = split_two(basis)
     width = high_ref.shape[2]
 
-    def step(c, _):
+    for c in range(high_ref.shape[0]):
         s, h = c // per_slice, c % per_slice
         high, low = high_ref[c], low_ref[c]
         value = jnp.dot(b_high, high, preferred_element_type=jnp.float32)
         value += jnp.dot(b_high, low, preferred_element_type=jnp.float32)
         value += jnp.dot(b_low, high, preferred_element_type=jnp.float32)
-        core_ref[s, :, pl.ds(pl.multiple_of(h * width, width), width)] = value
-        return 0
-
-    lax.fori_loop(0, high_ref.shape[0], step, 0)
+        core_ref[:, s, h * width:(h + 1) * width] = value
 
 
 def shards(nf, ng, tensor_slab, start_matrix):
@@ -350,14 +347,14 @@
         out_shape=(
             jax.ShapeDtypeStruct((modes, modes), jnp.float32),
             jax.ShapeDtypeStruct((modes, rank), jnp.float32),
-            jax.ShapeDtypeStruct((slices, rank, cells), jnp.float32),
+            jax.ShapeDtypeStruct((rank, slices, cells), jnp.float32),
         ),
         in_specs=[vmem] * 4,
         out_specs=(vmem, vmem, vmem),
-        scratch_shapes=[pltpu.VMEM((modes, modes), jnp.float32)],
+        scratch_shapes=[pltpu.VMEM((modes, modes), jnp.float32)] * 2,
         compiler_params=pltpu.CompilerParams(vmem_limit_bytes=56 * 1024 * 1024),
     )(start_matrix, gram, high, low)
-    return (triangle, basis, jnp.transpose(core, (1, 0, 2)))
+    return (triangle, basis, core)
 
 
 def solution(mesh):

time: 285 us -> 264 us (0.926)
  local copies, waits for them, and re-layouts: 18.5 us -> 0 us
    unnamed x2 -> x0, local copies, waits for them, and re-layouts: 15.7 us -> none
where the time goes in v3:
time: 264 us
  Pallas kernels  263 us (100%)
    pallas_call x1, Pallas kernels, exchange_and_gram(): pl.pallas_call(kernel, out_shape=(jax.ShapeDtypeStruct((chunks, modes, wi...  218 us
    pallas_call x1, Pallas kernels, shards(): pl.pallas_call(functools.partial(factor_kernel, cells // high.shape[2]),...  45.2 us

profile of v3, /device:TPU:1, one launch (start us, length us, event | category | flops | bytes accessed | tf_op | source)
XLA Modules:
  0.0 263.7 jit_solution(3439816698242254735)
XLA Ops:
  0.6 217.8 %shard_map.49 = (bf16[8,512,512]{2,1,0:T(8,128)(2,1)}, bf16[8,512,512]{2,1,0:T(8,128)(2,1)}, f32[1280,128]{1,0:T(8,128)}) custom-call(f32[64,32,1024]{2,1,0:T(8,128)} %x_ref.1), custom_call_target="tpu_custom_call" | custom-call | tf_op jit(solution)/shard_map/pallas_call | solution.py:199
  218.4 45.2 %shard_map.50 = (f32[512,512]{1,0:T(8,128)}, f32[512,128]{1,0:T(8,128)}, f32[128,4,1024]{2,1,0:T(4,128)}) custom-call(f32[512,128]{1,0:T(8,128)} %start_ref.1, f32[1280,128]{1,0:T(8,128)} %get-tuple-element.6.gram_ref, bf16[8,512,512]{2,1,0:T(8,128)(2,1)} %get-tuple-element.7.high_ref, bf16[8,512,512]{2,1,0:T(8,128)(2,1)} %get-tuple-element.8.low_ref), custom_call_target="tpu_custom_call" | custom-call | tf_op jit(solution)/shard_map/pallas_call | solution.py:345

commit v4 on v3

--- a/solution.py
+++ b/solution.py
@@ -96,23 +96,24 @@
 
     big = piece * nf
 
-    def group_copy(k):
+    def sub_piece(q):
+        return pl.multiple_of(lax.rem(mf + q, nf) * piece, 8)
+
+    def group_copy(k, q):
         peer = lax.rem(mg + k, ng)
         return pltpu.make_async_remote_copy(
-            src_ref=packed.at[pl.ds(pl.multiple_of(peer * big, 8), big), :],
-            dst_ref=group_in.at[k - 1],
-            send_sem=g_send.at[k - 1],
-            recv_sem=g_recv.at[k - 1],
+            src_ref=packed.at[pl.ds(pl.multiple_of(peer * big + sub_piece(q), 8), piece), :],
+            dst_ref=group_in.at[k - 1, pl.ds(sub_piece(q), piece), :],
+            send_sem=g_send.at[k - 1, q],
+            recv_sem=g_recv.at[k - 1, q],
             device_id=(mf, peer),
             device_id_type=MESH,
         )
 
-    for k in range(1, ng):
-        group_copy(k).start()
-    group_sum[...] = packed[pl.ds(pl.multiple_of(mg * big, 8), big), :]
-    for k in range(1, ng):
-        group_copy(k).wait_recv()
-        group_sum[...] += group_in[k - 1]
+    order = list(range(1, nf)) + [0]
+    for q in order:
+        for k in range(1, ng):
+            group_copy(k, q).start()
 
     def fiber_copy(k):
         peer = lax.rem(mf + k, nf)
@@ -125,8 +126,14 @@
             device_id_type=MESH,
         )
 
-    for k in range(1, nf):
-        fiber_copy(k).start()
+    for q in order:
+        value = packed[pl.ds(pl.multiple_of(mg * big + sub_piece(q), 8), piece), :]
+        for k in range(1, ng):
+            group_copy(k, q).wait_recv()
+            value += group_in[k - 1, pl.ds(sub_piece(q), piece), :]
+        group_sum[pl.ds(sub_piece(q), piece), :] = value
+        if q:
+            fiber_copy(q).start()
     total = group_sum[pl.ds(pl.multiple_of(mf * piece, 8), piece), :]
     for k in range(1, nf):
         fiber_copy(k).wait_recv()
@@ -144,26 +151,27 @@
             device_id_type=MESH,
         )
 
+    def group_gather(k, q):
+        part = pl.ds(pl.multiple_of(mg * big + lax.rem(mf - q + nf, nf) * piece, 8), piece)
+        return pltpu.make_async_remote_copy(
+            src_ref=gram_ref.at[part, :],
+            dst_ref=gram_ref.at[part, :],
+            send_sem=ga_send.at[k - 1, q],
+            recv_sem=ga_recv.at[k - 1, q],
+            device_id=(mf, lax.rem(mg + k, ng)),
+            device_id_type=MESH,
+        )
+
     for k in range(1, nf):
         fiber_gather(k).start()
-    for k in range(1, nf):
-        fiber_gather(k).wait_recv()
-
-    def group_gather(k):
-        part = pl.ds(pl.multiple_of(mg * big, 8), big)
-        return pltpu.make_async_remote_copy(
-            src_ref=gram_ref.at[part, :],
-            dst_ref=gram_ref.at[part, :],
-            send_sem=ga_send.at[k - 1],
-            recv_sem=ga_recv.at[k - 1],
-            device_id=(mf, lax.rem(mg + k, ng)),
-            device_id_type=MESH,
-        )
-
-    for k in range(1, ng):
-        group_gather(k).start()
-    for k in range(1, ng):
-        group_gather(k).wait_recv()
+    for q in range(nf):
+        if q:
+            fiber_gather(q).wait_recv()
+        for k in range(1, ng):
+            group_gather(k, q).start()
+    for q in range(nf):
+        for k in range(1, ng):
+            group_gather(k, q).wait_recv()
 
     def end_chunk(c, _):
         for k in range(1, nf):
@@ -172,8 +180,9 @@
 
     lax.fori_loop(0, chunks, end_chunk, 0)
     for k in range(1, ng):
-        group_copy(k).wait_send()
-        group_gather(k).wait_send()
+        for q in range(nf):
+            group_copy(k, q).wait_send()
+            group_gather(k, q).wait_send()
     for k in range(1, nf):
         fiber_copy(k).wait_send()
         fiber_gather(k).wait_send()
@@ -215,14 +224,14 @@
             dma((chunks,)),
             dma((nf - 1, chunks)),
             dma((nf - 1, chunks)),
-            dma((ng - 1,)),
-            dma((ng - 1,)),
+            dma((ng - 1, nf)),
+            dma((ng - 1, nf)),
             dma((nf - 1,)),
             dma((nf - 1,)),
             dma((nf - 1,)),
             dma((nf - 1,)),
-            dma((ng - 1,)),
-            dma((ng - 1,)),
+            dma((ng - 1, nf)),
+            dma((ng - 1, nf)),
         ],
         compiler_params=pltpu.CompilerParams(
             collective_id=0, has_side_effects=True, vmem_limit_bytes=56 * 1024 * 1024

time: 264 us -> 261 us (0.989)
  Pallas kernels: 263 us -> 259 us
    pallas_call x1, Pallas kernels: 218 us -> 214 us  [exchange_and_gram(): pl.pallas_call(kernel, out_shape=(jax.ShapeDtypeStruct((chunks, modes, wi...]
where the time goes in v4:
time: 261 us; the launch traced here: 260 us
  Pallas kernels  259 us (99%)
    pallas_call x1, Pallas kernels, exchange_and_gram(): pl.pallas_call(kernel, out_shape=(jax.ShapeDtypeStruct((chunks, modes, wi...  214 us
    pallas_call x1, Pallas kernels, shards(): pl.pallas_call(functools.partial(factor_kernel, cells // high.shape[2]),...  45.2 us

profile of v4, /device:TPU:1, one launch (start us, length us, event | category | flops | bytes accessed | tf_op | source)
XLA Modules:
  0.0 260.1 jit_solution(15341388120415668885)
XLA Ops:
  0.6 214.2 %shard_map.49 = (bf16[8,512,512]{2,1,0:T(8,128)(2,1)}, bf16[8,512,512]{2,1,0:T(8,128)(2,1)}, f32[1280,128]{1,0:T(8,128)}) custom-call(f32[64,32,1024]{2,1,0:T(8,128)} %x_ref.1), custom_call_target="tpu_custom_call" | custom-call | tf_op jit(solution)/shard_map/pallas_call | solution.py:208
  214.9 45.2 %shard_map.50 = (f32[512,512]{1,0:T(8,128)}, f32[512,128]{1,0:T(8,128)}, f32[128,4,1024]{2,1,0:T(4,128)}) custom-call(f32[512,128]{1,0:T(8,128)} %start_ref.1, f32[1280,128]{1,0:T(8,128)} %get-tuple-element.6.gram_ref, bf16[8,512,512]{2,1,0:T(8,128)(2,1)} %get-tuple-element.7.high_ref, bf16[8,512,512]{2,1,0:T(8,128)(2,1)} %get-tuple-element.8.low_ref), custom_call_target="tpu_custom_call" | custom-call | tf_op jit(solution)/shard_map/pallas_call | solution.py:354
